TPU v7x, 32 devices: a whole 2x2x4 slice. The times are simulated.
32 devices in a mesh: frame: 4 (over y, core), module: 8 (over z, x).
Axes of the slice: x: 2, y: 2, z: 4, core: 2. Of those that a mesh axis runs over, the one named last changes fastest.
Arguments:
- frames: bfloat16 [1024, 98304], P('frame', 'module'), may hold values from -6 to 6
- weights: bfloat16 [768, 512, 128], P('module'), may hold values from 0 to 0.25
- monitor: float32 [1024], P('frame'), may hold values from 0.5 to 2
- coverage: int32 [8, 96], replicated, may hold values from 0 to 255, as said below
- block_slot: int32 [8, 96], P('module'), may hold values from 0 to 95, each once within a row
- angle_index: int32 [2], replicated, may hold values from 0 to 179
Outputs:
- slices: bfloat16 [8, 4, 8, 128, 8192], P(None, 'frame', 'module')
Inputs may be any that keep to these rules, and one draw needn't show every extreme that they name: `coverage`: row m holds 96 consecutive tile numbers s, s + 1, ... taken modulo 256, in order, for a start s of its own. `block_slot`: each row is a permutation.
All inputs are finite; a program needn't handle non-finite values.
Results may differ from a plain program's by a relative error of at most 0.0055.
Values sent between devices are 32-bit elements; how exact they have to be, the bound alone decides.
A program may use at most 192 MiB of HBM per device.

v0:
```python
import math

import jax
import jax.numpy as jnp
from jax import lax
from jax.sharding import PartitionSpec as P

TRANS = 512
ASTEPS = 180
ROWS = 16
NTILE = 256


def ramp_table(length):
    places = jnp.arange(length, dtype=jnp.int32)
    offset = places[:, None] - places[None, :]
    is_odd = offset % 2 != 0
    scaled = math.pi * offset.astype(jnp.float32)
    safe_den = jnp.where(is_odd, scaled, jnp.float32(1.0))
    return jnp.where(
        offset == 0,
        jnp.float32(0.25),
        jnp.where(is_odd, -1.0 / (safe_den * safe_den), jnp.float32(0.0)),
    )


def spot_table(angle_index, row_count, length):
    theta_rad = angle_index.astype(jnp.float32) * (math.pi / ASTEPS)
    centre = (length - 1) / 2.0
    across = jnp.arange(length, dtype=jnp.float32) - centre
    down_pos = jnp.arange(row_count, dtype=jnp.float32) - (row_count - 1) / 2.0
    spot_grid = (
        across[None, None, :] * jnp.cos(theta_rad)[:, None, None]
        + down_pos[None, :, None] * jnp.sin(theta_rad)[:, None, None]
        + centre
    )
    return spot_grid.reshape(angle_index.shape[0], row_count * length)


def on_device(frames, weights, monitor, coverage, block_slot, angle_index):
    groups = lax.axis_size("frame")
    modules = lax.axis_size("module")
    module_pos = lax.axis_index("module")
    fr_dev, pixel_count = frames.shape
    slot_count, group_pixels, tile_width = weights.shape
    group_count = pixel_count // group_pixels
    splits = slot_count // group_count
    local_tiles = NTILE // modules
    per_peer = slot_count // modules
    grouped = frames.reshape(fr_dev, group_count, group_pixels)
    tile_weights = weights.reshape(group_count, splits, group_pixels, tile_width)
    block_bins = jnp.einsum(
        "fgp,gspc->gsfc", grouped, tile_weights, preferred_element_type=jnp.float32
    )
    block_bins = block_bins.reshape(slot_count, fr_dev, tile_width) / monitor[None, :, None]
    slot_rank = jnp.arange(slot_count, dtype=jnp.int32)
    own_slots = block_slot[0]
    slot_block = jnp.sum(
        jnp.where(own_slots[None, :] == slot_rank[:, None], slot_rank[None, :], 0), axis=1
    )
    first_tile = coverage[module_pos, 0]
    dest_order = jnp.arange(modules, dtype=jnp.int32)
    rounds = jnp.arange(per_peer, dtype=jnp.int32)
    send_slots = rounds[None, :] * modules + (dest_order[:, None] - first_tile) % modules
    outgoing = jnp.take(block_bins, slot_block[send_slots].reshape(-1), axis=0)
    outgoing = outgoing.reshape(modules, per_peer, fr_dev, tile_width)
    starts = coverage[:, 0]
    recv_slots = rounds[None, :] * modules + (module_pos - starts[:, None]) % modules
    recv_local = (starts[:, None] + recv_slots) % NTILE // modules
    gather_rows = (
        recv_local.reshape(1, -1) == jnp.arange(local_tiles, dtype=jnp.int32)[:, None]
    ).astype(jnp.float32)
    incoming = lax.all_to_all(outgoing, "module", split_axis=0, concat_axis=0, tiled=True)
    stacked_src = incoming.reshape(modules * per_peer, incoming.shape[2], tile_width)
    owned_bins = jnp.einsum(
        "lk,kfc->lfc", gather_rows, stacked_src, precision=lax.Precision.HIGHEST
    )
    tile_rounds = local_tiles // groups
    stacked = owned_bins.reshape(tile_rounds, groups, fr_dev, tile_width)
    angles = angle_index.shape[0]
    column_count = ROWS * TRANS
    ramp_filter = ramp_table(TRANS)
    spot_grid = spot_table(angle_index, ROWS, TRANS)
    positions = jnp.arange(TRANS, dtype=jnp.float32)

    def interp_rows(spot_line):
        return jnp.maximum(0.0, 1.0 - jnp.abs(spot_line[None, :] - positions[:, None])).astype(
            jnp.bfloat16
        )

    tables = lax.map(interp_rows, spot_grid)
    sinogram = lax.all_to_all(stacked, "frame", split_axis=1, concat_axis=2, tiled=True)
    item_count = sinogram.shape[0]
    sino_lines = sinogram.reshape(item_count, angles, TRANS, tile_width)
    filtered = jnp.einsum(
        "iapc,pq->aicq", sino_lines, ramp_filter, precision=lax.Precision.HIGHEST
    ).astype(jnp.bfloat16)
    filtered = filtered.reshape(angles, item_count * tile_width, TRANS)

    def add_angle(angle_pos, summed):
        angle_rows = lax.dynamic_index_in_dim(filtered, angle_pos, 0, keepdims=False)
        angle_table = lax.dynamic_index_in_dim(tables, angle_pos, 0, keepdims=False)
        return summed + jnp.dot(angle_rows, angle_table, preferred_element_type=jnp.float32)

    summed = lax.fori_loop(
        0, angles, add_angle, jnp.zeros((item_count * tile_width, column_count), jnp.float32)
    )
    slices = (summed * (math.pi / angles)).astype(jnp.bfloat16)
    return slices.reshape(item_count, 1, 1, tile_width, column_count)


def solution(mesh):
    placed = (
        P("frame", "module"),
        P("module", None, None),
        P("frame"),
        P(),
        P("module", None),
        P(),
    )
    return jax.shard_map(
        on_device,
        mesh=mesh,
        in_specs=placed,
        out_specs=P(None, "frame", "module", None, None),
        check_vma=False,
    )
```

profile of v0, /device:TPU:31, one launch (start us, length us, event | category | flops | bytes accessed | tf_op | source)
XLA Modules:
  0.0 498.0 jit_solution(8597004299137046794)
XLA Ops:
  0.0 1.2 constant_dynamic-slice_fusion.1
  1.2 0.7 and_select_fusion
  1.9 0.8 select_reduce_fusion
  2.6 0.1 compare_select_fusion.1
  2.7 0.1 reshape.356
  2.8 1.2 gather_fusion
  4.1 0.1 reshape.355
  4.2 8.3 %copy.29 = bf16[32,8,24,512]{3,2,1,0:T(8,128)(2,1)} copy(bf16[32,8,24,512]{3,1,2,0:T(8,128)(2,1)} %bitcast.58) | data formatting | bytes 12582912
  12.4 0.0 copy-start.1
  12.4 16.5 %fusion.15 = f32[24,4,128,256]{3,2,1,0:T(8,128)} fusion(bf16[24,4,512,128]{3,2,1,0:T(8,128)(2,1)} %bitcast.57, bf16[256,24,512,1]{2,1,0,3:T(8,128)(2,1)} %bitcast.55), kind=kOutput, calls=%fused_computation.21 | convolution fusion | flops 3221225472 | bytes 31457280 | tf_op jit(solution)/shard_map/fgp,gspc->gsfc/dot_general | solution.py:52
  28.9 0.0 copy-done.1
  28.9 11.3 %bitcast_divide_fusion = f32[96,256,128]{1,2,0:T(8,128)} fusion(f32[24,4,128,256]{3,2,1,0:T(8,128)} %fusion.15, f32[256]{0:T(256)S(1)} %copy-done.1), kind=kLoop, calls=%fused_computation.17 | loop fusion | flops 3145728 | bytes 25166848 | tf_op jit(solution)/shard_map/div | solution.py:55
  40.2 13.5 %gather_fusion.1 = f32[96,256,128]{1,2,0:T(8,128)} fusion(f32[96,256,128]{1,2,0:T(8,128)} %bitcast_divide_fusion, s32[1024]{0:T(1024)S(1)} %pad_clamp_fusion), kind=kCustom, calls=%fused_computation.1 | custom fusion | bytes 25166208 | tf_op jit(solution)/shard_map/jit(_take)/gather | solution.py:65
  53.7 12.6 %copy.19 = f32[96,256,128]{2,1,0:T(8,128)} copy(f32[96,256,128]{1,2,0:T(8,128)} %gather_fusion.1) | data formatting | bytes 25165824 | tf_op jit(solution)/shard_map/jit(_take)/gather | solution.py:65
  66.2 11.7 %broadcast_select_fusion = f32[8,12,256,128]{3,2,1,0:T(8,128)} fusion(f32[8,12,256,128]{3,2,1,0:T(8,128)} %bitcast.54, pred[8,12]{1,0:T(8,128)(4,1)S(1)} %compare_and_fusion), kind=kLoop, calls=%fused_computation.23 | loop fusion | flops 3145728 | bytes 25165920 | tf_op jit(solution)/shard_map/jit(_take)/select_n | solution.py:65
  78.0 0.0 copy-start
  78.0 0.0 copy-start.2
  78.0 5.6 %all-to-all-start = ((f32[8,12,256,128]{3,2,1,0:T(8,128)}), f32[8,12,256,128]{3,2,1,0:T(8,128)}, u32[]{:S(2)}, u32[]{:S(2)}) async-start(f32[8,12,256,128]{3,2,1,0:T(8,128)} %broadcast_select_fusion), calls=%async_computation | async-start | bytes 25165824 | tf_op jit(solution)/shard_map/all_to_all | solution.py:73
  83.6 0.0 copy-done
  83.6 0.1 slice_reduce_fusion
  83.7 0.1 add_add_fusion
  83.8 0.1 add.213
  83.9 0.0 copy-done.2
  83.9 0.1 broadcast_multiply_fusion.1
  84.0 0.1 broadcast_multiply_fusion
  84.1 0.1 add_bitcast_fusion
  84.2 0.1 copy.30
  84.3 270.7 %all-to-all-done = f32[8,12,256,128]{3,2,1,0:T(8,128)} async-done(((f32[8,12,256,128]{3,2,1,0:T(8,128)}), f32[8,12,256,128]{3,2,1,0:T(8,128)}, u32[]{:S(2)}, u32[]{:S(2)}) %all-to-all-start) | async-done | bytes 12582944 | tf_op jit(solution)/shard_map/all_to_all | solution.py:73
  355.0 16.9 %fusion.12 = f32[8,4,256,128]{3,0,2,1:T(8,128)} fusion(f32[96,256,128]{2,1,0:T(8,128)} %bitcast.13, s32[8,4]{0,1:T(4,128)S(1)} %multiply_add_fusion, s32[96]{0:T(128)S(1)} %and_select_fusion.1), kind=kOutput, calls=%fused_computation.18 | convolution fusion | flops 1207962624 | bytes 16777728 | tf_op jit(solution)/shard_map/lk,kfc->lfc/dot_general | solution.py:75
  371.9 5.4 %all-to-all-start.1 = ((f32[8,4,256,128]{3,0,2,1:T(8,128)}), f32[8,4,256,128]{3,0,2,1:T(8,128)}, u32[]{:S(2)}, u32[]{:S(2)}) async-start(f32[8,4,256,128]{3,0,2,1:T(8,128)} %fusion.12), calls=%async_computation.1 | async-start | bytes 8388608 | tf_op jit(solution)/shard_map/all_to_all | solution.py:92
  377.3 12.5 %while.25 = (s32[]{:T(128)}, bf16[2,512,8192]{2,1,0:T(8,128)(2,1)}, f32[2,8192]{1,0:T(2,128)S(1)}, s32[]{:T(128)}) while((s32[]{:T(128)}, bf16[2,512,8192]{2,1,0:T(8,128)(2,1)}, f32[2,8192]{1,0:T(2,128)S(1)}, s32[]{:T(128)}) %tuple.57), condition=%wide.region_2.3_spmd.clone, body=%wide.region_1.2_spmd.clone.sunk | while | flops 20971520 | bytes 8486981 | solution.py:91
  377.4 6.2 %fusion.70 = bf16[2,512,8192]{2,1,0:T(8,128)(2,1)} fusion(bf16[2,512,8192]{2,1,0:T(8,128)(2,1)} %get-tuple-element.198, s32[]{:T(128)S(6)} %copy.44, f32[8192]{0:T(1024)S(1)} %bitcast.59), kind=kLoop, calls=%fused_computation.8.clone.1 | loop fusion | flops 20971520 | bytes 8421380 | tf_op jit(solution)/shard_map/while/body/jit(dynamic_update_index_in_dim)/dynamic_update_slice | solution.py:91
  383.6 6.2 %fusion.70 = bf16[2,512,8192]{2,1,0:T(8,128)(2,1)} fusion(bf16[2,512,8192]{2,1,0:T(8,128)(2,1)} %get-tuple-element.198, s32[]{:T(128)S(6)} %copy.44, f32[8192]{0:T(1024)S(1)} %bitcast.59), kind=kLoop, calls=%fused_computation.8.clone.1 | loop fusion | flops 20971520 | bytes 8421380 | tf_op jit(solution)/shard_map/while/body/jit(dynamic_update_index_in_dim)/dynamic_update_slice | solution.py:91
  389.8 33.7 %all-to-all-done.1 = f32[8,4,256,128]{3,0,2,1:T(8,128)} async-done(((f32[8,4,256,128]{3,0,2,1:T(8,128)}), f32[8,4,256,128]{3,0,2,1:T(8,128)}, u32[]{:S(2)}, u32[]{:S(2)}) %all-to-all-start.1) | async-done | bytes 4194336 | tf_op jit(solution)/shard_map/all_to_all | solution.py:92
  423.5 10.0 %convert_bitcast_fusion = bf16[2,8,128,512]{3,2,0,1:T(8,128)(2,1)S(1)} fusion(f32[8,2,512,128]{3,0,2,1:T(8,128)} %bitcast.15), kind=kOutput, calls=%fused_computation.26 | convolution fusion | flops 6449004544 | bytes 6291456 | tf_op jit(solution)/shard_map/iapc,pq->aicq/dot_general | solution.py:95
  433.6 0.2 copy.22
  433.8 46.5 %while.26 = (s32[]{:T(128)}, f32[1024,8192]{1,0:T(8,128)}, bf16[2,1024,512]{2,1,0:T(8,128)(2,1)S(1)}, bf16[2,512,8192]{2,1,0:T(8,128)(2,1)}, s32[]{:T(128)}, /*index=5*/s32[]{:T(128)}) while((s32[]{:T(128)}, f32[1024,8192]{1,0:T(8,128)}, bf16[2,1024,512]{2,1,0:T(8,128)(2,1)S(1)}, bf16[2,512,8192]{2,1,0:T(8,128)(2,1)}, s32[]{:T(128)}, ...), condition=%wide.region_4.5_spmd.clone, body=%wide.region_3.4_spmd.clone.sunk | while | flops 8606711808 | bytes 76547672 | solution.py:105
  433.8 17.9 %select_add_fusion.2 = f32[1024,8192]{1,0:T(8,128)} fusion(f32[1024,8192]{1,0:T(8,128)} %get-tuple-element.212, pred[]{:T(512)S(6)} %compare.20, bf16[2,512,8192]{2,1,0:T(8,128)(2,1)} %get-tuple-element.220, s32[]{:T(128)S(6)} %copy.50, bf16[2,1024,512]{2,1,0:T(8,128)(2,1)S(1)} %get-tuple-element.219), kind=kOutput, calls=%fused_computation.10.clone.1 | convolution fusion | flops 8606711808 | bytes 76547584 | tf_op jit(solution)/shard_map/while/body/eval_jaxpr/dot_general | solution.py:103
  451.7 28.6 %select_add_fusion.2 = f32[1024,8192]{1,0:T(8,128)} fusion(f32[1024,8192]{1,0:T(8,128)} %get-tuple-element.212, pred[]{:T(512)S(6)} %compare.20, bf16[2,512,8192]{2,1,0:T(8,128)(2,1)} %get-tuple-element.220, s32[]{:T(128)S(6)} %copy.50, bf16[2,1024,512]{2,1,0:T(8,128)(2,1)S(1)} %get-tuple-element.219), kind=kOutput, calls=%fused_computation.10.clone.1 | convolution fusion | flops 8606711808 | bytes 76547584 | tf_op jit(solution)/shard_map/while/body/eval_jaxpr/dot_general | solution.py:103
  480.2 17.8 %multiply_convert_fusion = bf16[1024,8192]{1,0:T(8,128)(2,1)} fusion(f32[1024,8192]{1,0:T(8,128)} %get-tuple-element.107), kind=kLoop, calls=%fused_computation.16 | loop fusion | flops 16777216 | bytes 50331648 | tf_op jit(solution)/shard_map/convert_element_type | solution.py:108
  (14 shorter events, 0.2 us)
Async XLA Ops:
  12.4 16.5 %copy-start.1 = (f32[256]{0:T(256)S(1)}, f32[256]{0:T(256)}, u32[]{:S(2)}) copy-start(f32[256]{0:T(256)} %param.12) | copy-start | bytes 3076
  78.0 5.6 %copy-start = (s32[8,96]{1,0:T(8,128)S(1)}, s32[8,96]{1,0:T(8,128)}, u32[]{:S(2)}) copy-start(s32[8,96]{1,0:T(8,128)} %param.13) | copy-start | bytes 9220
  78.0 5.9 %copy-start.2 = (s32[2]{0:T(128)S(1)}, s32[2]{0:T(128)}, u32[]{:S(2)}) copy-start(s32[2]{0:T(128)} %param.15) | copy-start | bytes 28
  78.0 277.0 %all-to-all-start = ((f32[8,12,256,128]{3,2,1,0:T(8,128)}), f32[8,12,256,128]{3,2,1,0:T(8,128)}, u32[]{:S(2)}, u32[]{:S(2)}) async-start(f32[8,12,256,128]{3,2,1,0:T(8,128)} %broadcast_select_fusion), calls=%async_computation | async-start | bytes 25165824 | tf_op jit(solution)/shard_map/all_to_all | solution.py:73
  371.9 51.7 %all-to-all-start.1 = ((f32[8,4,256,128]{3,0,2,1:T(8,128)}), f32[8,4,256,128]{3,0,2,1:T(8,128)}, u32[]{:S(2)}, u32[]{:S(2)}) async-start(f32[8,4,256,128]{3,0,2,1:T(8,128)} %fusion.12), calls=%async_computation.1 | async-start | bytes 8388608 | tf_op jit(solution)/shard_map/all_to_all | solution.py:92
where the time goes:
time: 504 us; the launch traced here: 498 us
  waiting for transfers between devices  304 us (60%)
  matrix products  89.8 us (18%)
  other arithmetic  55.2 us (11%)
  local copies, waits for them, and re-layouts  37.3 us (7%)
  starting transfers between devices  11 us (2%)
    all_to_all x1, waiting for transfers between devices, on_device(): lax.all_to_all(outgoing, 'module', split_axis=0, concat_axis=0, tiled=True)  271 us
    dot_general x2, matrix products, add_angle(): jnp.dot(angle_rows, angle_table, preferred_element_type=jnp.float32)  46.5 us
    all_to_all x1, waiting for transfers between devices, on_device(): lax.all_to_all(stacked, 'frame', split_axis=1, concat_axis=2, tiled=True)  33.7 us
    gather x4, local copies, waits for them, and re-layouts, on_device(): outgoing = jnp.take(block_bins, slot_block[send_slots].reshape(-1), axis=0)  27.4 us
    convert_element_type x1, other arithmetic, on_device(): slices = (summed * (math.pi / angles)).astype(jnp.bfloat16)  17.8 us
    dot_general x1, matrix products, on_device(): jnp.einsum('lk,kfc->lfc', gather_rows, stacked_src, precision=lax.Precisi...  16.9 us
    dot_general x1, matrix products, on_device(): jnp.einsum('fgp,gspc->gsfc', grouped, tile_weights, preferred_element_typ...  16.5 us
    dynamic_update_slice x2, other arithmetic, on_device(): tables = lax.map(interp_rows, spot_grid)  12.4 us
  transfers between devices with their start and end apart: 2, of which 2 were waited for; matrix products, arithmetic and copies ran while one was open for 3% of the time, Pallas kernels for 0%

commit v1 on v0

v1 whole, which is shorter than its diff:
```python
import functools
import math

import jax
import jax.numpy as jnp
from jax import lax
from jax.experimental import pallas as pl
from jax.experimental.pallas import tpu as pltpu
from jax.sharding import PartitionSpec as P

TRANS = 512
ASTEPS = 180
ROWS = 16
NTILE = 256
MIB = 1024 * 1024


def ramp_table(length):
    places = jnp.arange(length, dtype=jnp.int32)
    offset = places[:, None] - places[None, :]
    is_odd = offset % 2 != 0
    scaled = math.pi * offset.astype(jnp.float32)
    safe_den = jnp.where(is_odd, scaled, jnp.float32(1.0))
    return jnp.where(
        offset == 0,
        jnp.float32(0.25),
        jnp.where(is_odd, -1.0 / (safe_den * safe_den), jnp.float32(0.0)),
    )


def spot_table(angle_index, row_count, length):
    theta_rad = angle_index.astype(jnp.float32) * (math.pi / ASTEPS)
    centre = (length - 1) / 2.0
    across = jnp.arange(length, dtype=jnp.float32) - centre
    down_pos = jnp.arange(row_count, dtype=jnp.float32) - (row_count - 1) / 2.0
    spot_grid = (
        across[None, None, :] * jnp.cos(theta_rad)[:, None, None]
        + down_pos[None, :, None] * jnp.sin(theta_rad)[:, None, None]
        + centre
    )
    return spot_grid.reshape(angle_index.shape[0], row_count * length)


def plane_of(modules):
    wide = max(w for w in range(1, modules + 1) if modules % w == 0 and w * w <= modules)
    return modules // wide, wide


def split_kernel(splits, place_ref, frames_ref, weights_ref, monitor_ref, out_ref):
    group = pl.program_id(0)
    scale = 1.0 / monitor_ref[...]
    for part in range(splits):
        bins = jnp.dot(frames_ref[...], weights_ref[part], preferred_element_type=jnp.float32)
        out_ref[place_ref[group * splits + part]] = bins * scale


def split(frames, weights, monitor, places):
    fr_dev, pixel_count = frames.shape
    slot_count, group_pixels, tile_width = weights.shape
    group_count = pixel_count // group_pixels
    splits = slot_count // group_count
    return pl.pallas_call(
        functools.partial(split_kernel, splits),
        out_shape=jax.ShapeDtypeStruct((slot_count, fr_dev, tile_width), jnp.float32),
        grid_spec=pltpu.PrefetchScalarGridSpec(
            num_scalar_prefetch=1,
            grid=(group_count,),
            in_specs=[
                pl.BlockSpec((fr_dev, group_pixels), lambda g, _: (0, g)),
                pl.BlockSpec((splits, group_pixels, tile_width), lambda g, _: (g, 0, 0)),
                pl.BlockSpec((fr_dev, 1), lambda g, _: (0, 0)),
            ],
            out_specs=pl.BlockSpec((slot_count, fr_dev, tile_width), lambda g, _: (0, 0, 0)),
        ),
        compiler_params=pltpu.CompilerParams(vmem_limit_bytes=48 * MIB),
        cost_estimate=pl.CostEstimate(
            flops=2 * fr_dev * slot_count * group_pixels * tile_width,
            bytes_accessed=frames.size * 2 + weights.size * 2 + slot_count * fr_dev * tile_width * 4,
            transcendentals=0,
        ),
    )(places, frames, weights, monitor[:, None])


def exchange_kernel(
    plan, rank_ref, bins_ref, out_ref,
    merge_in, owner_in, dense_out, dense_in, owned, merge_work, owner_work,
    merge_send, merge_recv, owner_send, owner_recv, dense_send, dense_recv,
    frame_send, frame_recv, local_sem,
):
    groups, modules, deep, wide, chunks, rows, per_peer, local_tiles = plan
    deep_half = deep // 2
    sources = deep_half * wide
    fr_dev = chunks * rows
    frame_pos = lax.axis_index("frame")
    module_pos = lax.axis_index("module")
    z_pos, x_pos = module_pos // wide, module_pos % wide
    half = z_pos // deep_half
    first_z, other_z = half * deep_half, (1 - half) * deep_half
    place = (z_pos - first_z) * wide + x_pos
    merge_z = jnp.where(half == 0, deep_half - 1, deep_half)
    merges = z_pos == merge_z

    barrier = pltpu.get_barrier_semaphore()
    for step in range(1, modules):
        pl.semaphore_signal(
            barrier, inc=1, device_id=(frame_pos, lax.rem(module_pos + step, modules)),
            device_id_type=pl.DeviceIdType.MESH,
        )
    for step in range(1, groups):
        pl.semaphore_signal(
            barrier, inc=1, device_id=(lax.rem(frame_pos + step, groups), module_pos),
            device_id_type=pl.DeviceIdType.MESH,
        )
    pl.semaphore_wait(barrier, modules + groups - 2)

    def chunk_of(c):
        return pl.ds(pl.multiple_of(c * rows, rows), rows)

    def remote(src, dst, send, recv, frame, module):
        return pltpu.make_async_remote_copy(
            src_ref=src, dst_ref=dst, send_sem=send, recv_sem=recv,
            device_id=(frame, module), device_id_type=pl.DeviceIdType.MESH,
        )

    def merge_copy(c, target_x, source):
        return remote(
            bins_ref.at[target_x, pl.ds(other_z, deep_half), :, chunk_of(c), :],
            merge_in.at[source, :, :, chunk_of(c), :],
            merge_send.at[target_x, c], merge_recv.at[source, c],
            frame_pos, merge_z * wide + target_x,
        )

    def owner_copy(c, target, source):
        target_z, target_x = first_z + target // wide, target % wide
        return remote(
            bins_ref.at[target_x, target_z, :, chunk_of(c), :],
            owner_in.at[source, :, chunk_of(c), :],
            owner_send.at[target, c], owner_recv.at[source, c],
            frame_pos, target_z * wide + target_x,
        )

    def dense_copy(c, i):
        return remote(
            dense_out.at[i, :, chunk_of(c), :], dense_in.at[:, chunk_of(c), :],
            dense_send.at[i, c], dense_recv.at[c],
            frame_pos, (other_z + i) * wide + x_pos,
        )

    def frame_copy(c, target, source):
        start = pl.multiple_of(source * fr_dev + c * rows, rows)
        return remote(
            owned.at[target, :, chunk_of(c), :], out_ref.at[:, pl.ds(start, rows), :],
            frame_send.at[target, c], frame_recv.at[source, c],
            target, module_pos,
        )

    def own_merge():
        return pltpu.make_async_copy(
            bins_ref.at[x_pos, pl.ds(other_z, deep_half)], merge_in.at[place], local_sem.at[0]
        )

    def own_owner():
        return pltpu.make_async_copy(
            bins_ref.at[x_pos, z_pos], owner_in.at[place], local_sem.at[1]
        )

    def own_frame(c):
        start = pl.multiple_of(frame_pos * fr_dev + c * rows, rows)
        return pltpu.make_async_copy(
            owned.at[frame_pos, :, chunk_of(c), :], out_ref.at[:, pl.ds(start, rows), :],
            frame_recv.at[frame_pos, c],
        )

    def start_merge(c):
        for target_x in range(wide):
            @pl.when(jnp.logical_not(merges & (x_pos == target_x)))
            def _():
                merge_copy(c, target_x, place).start()

    def sent_merge(c):
        for target_x in range(wide):
            @pl.when(jnp.logical_not(merges & (x_pos == target_x)))
            def _():
                merge_copy(c, target_x, place).wait_send()

    def start_owner(c):
        for target in range(sources):
            @pl.when(place != target)
            def _():
                owner_copy(c, target, place).start()

    def sent_owner(c):
        for target in range(sources):
            @pl.when(place != target)
            def _():
                owner_copy(c, target, place).wait_send()

    ahead = min(2, chunks)
    for c in range(ahead):
        start_merge(c)

    @pl.when(merges)
    def _():
        own_merge().start()

    own_owner().start()

    @pl.when(merges)
    def _():
        own_merge().wait()

    def pick(buffer_at, row):
        rank = rank_ref[row]
        value = buffer_at(jnp.maximum(rank, 0))
        return value * (rank >= 0).astype(jnp.float32)

    def merge_step(c, _):
        @pl.when(merges)
        def _():
            for source in range(sources):
                @pl.when(place != source)
                def _():
                    merge_copy(c, 0, source).wait_recv()

            for source in range(sources):
                merge_work[source] = merge_in[source, :, :, chunk_of(c), :]

            def merge_tile(l, _):
                for i in range(deep_half):
                    total = None
                    for source in range(sources):
                        term = pick(
                            lambda r: merge_work[source, i, r],
                            (source * (deep_half + 1) + 1 + i) * local_tiles + l,
                        )
                        total = term if total is None else total + term
                    dense_out[i, l, chunk_of(c), :] = total
                return 0

            lax.fori_loop(0, local_tiles, merge_tile, 0)
            for i in range(deep_half):
                dense_copy(c, i).start()

        sent_merge(c)

        @pl.when(c + ahead < chunks)
        def _():
            start_merge(c + ahead)

        return 0

    lax.fori_loop(0, chunks, merge_step, 0)

    for c in range(ahead):
        start_owner(c)
    own_owner().wait()

    def owner_step(c, _):
        for source in range(sources):
            @pl.when(place != source)
            def _():
                owner_copy(c, 0, source).wait_recv()

        dense_copy(c, 0).wait_recv()

        for source in range(sources):
            owner_work[source] = owner_in[source, :, chunk_of(c), :]

        def owner_tile(q, _):
            for f in range(groups):
                l = q * groups + f
                total = dense_in[l, chunk_of(c), :]
                for source in range(sources):
                    total = total + pick(
                        lambda r: owner_work[source, r],
                        source * (deep_half + 1) * local_tiles + l,
                    )
                owned[f, q, chunk_of(c), :] = total
            return 0

        lax.fori_loop(0, local_tiles // groups, owner_tile, 0)
        for f in range(groups):
            @pl.when(frame_pos != f)
            def _():
                frame_copy(c, f, frame_pos).start()

        own_frame(c).start()
        sent_owner(c)

        @pl.when(c + ahead < chunks)
        def _():
            start_owner(c + ahead)

        return 0

    lax.fori_loop(0, chunks, owner_step, 0)

    def finish(c, _):
        @pl.when(merges)
        def _():
            for i in range(deep_half):
                dense_copy(c, i).wait_send()

        for f in range(groups):
            @pl.when(frame_pos != f)
            def _():
                frame_copy(c, f, frame_pos).wait_send()
                frame_copy(c, f, f).wait_recv()

        own_frame(c).wait()
        return 0

    lax.fori_loop(0, chunks, finish, 0)


def exchange(bins, ranks, groups, modules, local_tiles, chunks):
    wide, deep, per_peer, fr_dev, width = bins.shape
    deep_half = deep // 2
    sources = deep_half * wide
    rows = fr_dev // chunks
    plan = (groups, modules, deep, wide, chunks, rows, per_peer, local_tiles)
    dma = pltpu.SemaphoreType.DMA
    return pl.pallas_call(
        functools.partial(exchange_kernel, plan),
        out_shape=jax.ShapeDtypeStruct((local_tiles // groups, groups * fr_dev, width), jnp.float32),
        in_specs=[
            pl.BlockSpec(memory_space=pltpu.SMEM),
            pl.BlockSpec(memory_space=pl.ANY),
        ],
        out_specs=pl.BlockSpec(memory_space=pl.ANY),
        scratch_shapes=[
            pltpu.VMEM((sources, deep_half, per_peer, fr_dev, width), jnp.float32),
            pltpu.VMEM((sources, per_peer, fr_dev, width), jnp.float32),
            pltpu.VMEM((deep_half, local_tiles, fr_dev, width), jnp.float32),
            pltpu.VMEM((local_tiles, fr_dev, width), jnp.float32),
            pltpu.VMEM((groups, local_tiles // groups, fr_dev, width), jnp.float32),
            pltpu.VMEM((sources, deep_half, per_peer, rows, width), jnp.float32),
            pltpu.VMEM((sources, per_peer, rows, width), jnp.float32),
            dma((wide, chunks)),
            dma((sources, chunks)),
            dma((sources, chunks)),
            dma((sources, chunks)),
            dma((deep_half, chunks)),
            dma((chunks,)),
            dma((groups, chunks)),
            dma((groups, chunks)),
            dma((2,)),
        ],
        compiler_params=pltpu.CompilerParams(
            collective_id=0, has_side_effects=True, vmem_limit_bytes=48 * MIB
        ),
        cost_estimate=pl.CostEstimate(
            flops=bins.size, bytes_accessed=bins.size * 8, transcendentals=0
        ),
    )(ranks, bins)


def project_kernel(angles, items, sino_ref, ramp_ref, spot_ref, out_ref, filtered):
    length = ramp_ref.shape[0]
    width = sino_ref.shape[2]

    @pl.when(pl.program_id(0) == 0)
    def _():
        def filter_item(item, _):
            for angle in range(angles):
                lines = sino_ref[item, angle * length : (angle + 1) * length, :]
                line_rows = lax.dot_general(
                    lines.T, ramp_ref[...], (((1,), (0,)), ((), ())),
                    precision=lax.Precision.HIGHEST, preferred_element_type=jnp.float32,
                )
                filtered[
                    pl.ds(pl.multiple_of(item * width, width), width),
                    angle * length : (angle + 1) * length,
                ] = line_rows.astype(jnp.bfloat16)
            return 0

        lax.fori_loop(0, items, filter_item, 0)

    columns = out_ref.shape[2]
    positions = lax.broadcasted_iota(jnp.int32, (length, columns), 0).astype(jnp.float32)
    total = None
    for angle in range(angles):
        table = jnp.maximum(
            0.0, 1.0 - jnp.abs(spot_ref[angle : angle + 1, :] - positions)
        ).astype(jnp.bfloat16)
        part = jnp.dot(
            filtered[:, angle * length : (angle + 1) * length], table,
            preferred_element_type=jnp.float32,
        )
        total = part if total is None else total + part
    out_ref[...] = (total * (math.pi / angles)).astype(jnp.bfloat16).reshape(out_ref.shape)


def project(sinogram, ramp_filter, spot_grid):
    items, frame_count, width = sinogram.shape
    angles, column_count = spot_grid.shape
    length = ramp_filter.shape[0]
    block = length
    return pl.pallas_call(
        functools.partial(project_kernel, angles, items),
        out_shape=jax.ShapeDtypeStruct((items, width, column_count), jnp.bfloat16),
        grid=(column_count // block,),
        in_specs=[
            pl.BlockSpec((items, frame_count, width), lambda j: (0, 0, 0)),
            pl.BlockSpec((length, length), lambda j: (0, 0)),
            pl.BlockSpec((angles, block), lambda j: (0, j)),
        ],
        out_specs=pl.BlockSpec((items, width, block), lambda j: (0, 0, j)),
        scratch_shapes=[pltpu.VMEM((items * width, frame_count), jnp.bfloat16)],
        compiler_params=pltpu.CompilerParams(vmem_limit_bytes=48 * MIB),
        cost_estimate=pl.CostEstimate(
            flops=2 * items * width * frame_count * column_count,
            bytes_accessed=sinogram.size * 4 + items * width * column_count * 2,
            transcendentals=0,
        ),
    )(sinogram, ramp_filter, spot_grid)


def on_device(frames, weights, monitor, coverage, block_slot, angle_index):
    groups = lax.axis_size("frame")
    modules = lax.axis_size("module")
    module_pos = lax.axis_index("module")
    deep, wide = plane_of(modules)
    fr_dev = frames.shape[0]
    slot_count, _, tile_width = weights.shape
    local_tiles = NTILE // modules
    per_peer = slot_count // modules
    starts = coverage[:, 0]

    own_slots = block_slot[0]
    owner = (starts[module_pos] + own_slots) % modules
    places = ((owner % wide) * deep + owner // wide) * per_peer + own_slots // modules
    bins = split(frames, weights, monitor, places)
    bins = bins.reshape(wide, deep, per_peer, fr_dev, tile_width)

    deep_half = deep // 2
    z_pos, x_pos = module_pos // wide, module_pos % wide
    half = z_pos // deep_half
    source_module = half * deep_half * wide + jnp.arange(deep_half * wide, dtype=jnp.int32)
    target_module = jnp.concatenate([
        module_pos[None],
        ((1 - half) * deep_half + jnp.arange(deep_half, dtype=jnp.int32)) * wide + x_pos,
    ])
    tiles = (
        jnp.arange(local_tiles, dtype=jnp.int32)[None, None, :] * modules
        + target_module[None, :, None]
    )
    slots = (tiles - starts[source_module][:, None, None]) % NTILE
    ranks = jnp.where(slots < slot_count, slots // modules, -1).reshape(-1)
    sinogram = exchange(bins, ranks, groups, modules, local_tiles, 8)

    slices = project(sinogram, ramp_table(TRANS), spot_table(angle_index, ROWS, TRANS))
    return slices.reshape(slices.shape[0], 1, 1, tile_width, ROWS * TRANS)


def solution(mesh):
    placed = (
        P("frame", "module"),
        P("module", None, None),
        P("frame"),
        P(),
        P("module", None),
        P(),
    )
    return jax.shard_map(
        on_device,
        mesh=mesh,
        in_specs=placed,
        out_specs=P(None, "frame", "module", None, None),
        check_vma=False,
    )
```

time: 504 us -> 316 us (0.63)
  Pallas kernels: 0 us -> 309 us
  waiting for transfers between devices: 304 us -> 0 us
  matrix products: 89.8 us -> 0 us
  other arithmetic: 55.2 us -> 3.07 us
  local copies, waits for them, and re-layouts: 37.3 us -> 2.91 us
  starting transfers between devices: 11 us -> 0 us
    pallas_call x0 -> x3, Pallas kernels: none -> 309 us  [the longest x1 252 us: exchange(): pl.pallas_call(functools.partial(exchange_kernel, plan), out_shape=jax.Sh...]
    all_to_all x2 -> x0, waiting for transfers between devices: 304 us -> none  [the longest x1 271 us: on_device(): lax.all_to_all(outgoing, 'module', split_axis=0, concat_axis=0, tiled=True)]
    dot_general x5 -> x0, matrix products: 89.8 us -> none  [the longest x2 46.5 us: add_angle(): jnp.dot(angle_rows, angle_table, preferred_element_type=jnp.float32)]
    gather x4 -> x1, local copies, waits for them, and re-layouts: 27.4 us -> 0.64 us  [on_device(): slots = (tiles - starts[source_module][:, None, None]) % NTILE]
    convert_element_type x1 -> x0, other arithmetic: 17.8 us -> none  [on_device(): slices = (summed * (math.pi / angles)).astype(jnp.bfloat16)]
    dynamic_update_slice x2 -> x0, other arithmetic: 12.4 us -> none  [on_device(): tables = lax.map(interp_rows, spot_grid)]
    select_n x5 -> x3, other arithmetic: 12.5 us -> 0.58 us  [the longest x1 0.56 us: ramp_table(): jnp.where(offset == 0, jnp.float32(0.25), jnp.where(is_odd, -1.0 / (safe_...]
    div x1 -> x0, other arithmetic: 11.3 us -> none  [on_device(): block_bins.reshape(slot_count, fr_dev, tile_width) / monitor[None, :, None]]
  transfers between devices with their start and end apart: 2 -> 0, of which waited for: 2 -> 0; matrix products, arithmetic and copies ran while one was open for 3% -> 0% of each run, Pallas kernels for 0% -> 0%
where the time goes in v1:
time: 316 us; the launch traced here: 315 us
  Pallas kernels  309 us (98%)
    pallas_call x1, Pallas kernels, exchange(): pl.pallas_call(functools.partial(exchange_kernel, plan), out_shape=jax.Sh...  252 us
    pallas_call x1, Pallas kernels, project(): pl.pallas_call(functools.partial(project_kernel, angles, items), out_shap...  31.8 us
    pallas_call x1, Pallas kernels, split(): pl.pallas_call(functools.partial(split_kernel, splits), out_shape=jax.Sha...  25 us

profile of v1, /device:TPU:31, one launch (start us, length us, event | category | flops | bytes accessed | tf_op | source)
XLA Modules:
  0.0 315.0 jit_solution(14961230395387840440)
XLA Ops:
  0.0 0.1 pad_add_fusion
  0.1 0.1 broadcast_add_fusion
  0.2 0.7 fusion.16
  0.9 0.1 broadcast_multiply_fusion.1
  1.0 0.1 broadcast_multiply_fusion
  1.0 0.8 fusion.17
  1.8 0.6 gather_fusion
  2.5 0.5 constant_dynamic-slice_fusion
  3.0 1.3 fusion.14.place_ref
  4.3 0.1 broadcast_subtract_fusion
  4.4 0.1 sub.69
  4.5 0.1 add_bitcast_fusion
  4.6 0.1 copy.10
  4.6 0.8 copy.8.monitor_ref
  5.4 0.6 select_select_fusion.ramp_ref
  6.0 25.0 %shard_map.64 = f32[96,256,128]{2,1,0:T(8,128)} custom-call(s32[96]{0:T(128)S(1)} %fusion.14.place_ref, bf16[256,12288]{1,0:T(8,128)(2,1)} %frames_ref.1, bf16[96,512,128]{2,1,0:T(8,128)(2,1)} %weights_ref.1, f32[256,1]{1,0:T(8,128)S(1)} %copy.8.monitor_ref), custom_call_target="tpu_custom_call" | custom-call | flops 3221225472 | bytes 31457280 | tf_op jit(solution)/shard_map/pallas_call | solution.py:62
  31.1 252.1 %shard_map.65.sino_ref = f32[8,1024,128]{2,1,0:T(8,128)S(1)} custom-call(s32[384]{0:T(512)S(1)} %fusion.8.rank_ref, f32[2,4,12,256,128]{4,3,2,1,0:T(8,128)} %bitcast.28), custom_call_target="tpu_custom_call" | custom-call | flops 3145728 | bytes 25165824 | tf_op jit(solution)/shard_map/pallas_call | solution.py:323
  283.1 31.8 %shard_map.66 = bf16[8,128,8192]{2,1,0:T(8,128)(2,1)} custom-call(f32[8,1024,128]{2,1,0:T(8,128)S(1)} %shard_map.65.sino_ref, f32[512,512]{1,0:T(8,128)S(1)} %select_select_fusion.ramp_ref, f32[2,8192]{1,0:T(2,128)S(1)} %bitcast.27), custom_call_target="tpu_custom_call" | custom-call | flops 17179869184 | bytes 20971520 | tf_op jit(solution)/shard_map/pallas_call | solution.py:399
  (7 shorter events, 0.1 us)

commit v2 on v1

--- a/solution.py
+++ b/solution.py
@@ -49,9 +49,13 @@
 def split_kernel(splits, place_ref, frames_ref, weights_ref, monitor_ref, out_ref):
     group = pl.program_id(0)
     scale = 1.0 / monitor_ref[...]
+    tile_width = weights_ref.shape[2]
+    joined = jnp.concatenate([weights_ref[part] for part in range(splits)], axis=1)
+    bins = jnp.dot(frames_ref[...], joined, preferred_element_type=jnp.float32)
     for part in range(splits):
-        bins = jnp.dot(frames_ref[...], weights_ref[part], preferred_element_type=jnp.float32)
-        out_ref[place_ref[group * splits + part]] = bins * scale
+        out_ref[place_ref[group * splits + part]] = (
+            bins[:, part * tile_width : (part + 1) * tile_width] * scale
+        )
 
 
 def split(frames, weights, monitor, places):
@@ -217,6 +221,7 @@
     def merge_step(c, _):
         @pl.when(merges)
         def _():
+            start_owner(c)
             for source in range(sources):
                 @pl.when(place != source)
                 def _():
@@ -251,8 +256,11 @@
 
     lax.fori_loop(0, chunks, merge_step, 0)
 
-    for c in range(ahead):
-        start_owner(c)
+    @pl.when(jnp.logical_not(merges))
+    def _():
+        for c in range(ahead):
+            start_owner(c)
+
     own_owner().wait()
 
     def owner_step(c, _):
@@ -287,7 +295,7 @@
         own_frame(c).start()
         sent_owner(c)
 
-        @pl.when(c + ahead < chunks)
+        @pl.when(jnp.logical_not(merges) & (c + ahead < chunks))
         def _():
             start_owner(c + ahead)
 
@@ -355,26 +363,30 @@
     )(ranks, bins)
 
 
-def project_kernel(angles, items, sino_ref, ramp_ref, spot_ref, out_ref, filtered):
+def project_kernel(angles, items, sino_ref, ramp_ref, spot_ref, out_ref, filtered, high, low):
     length = ramp_ref.shape[0]
     width = sino_ref.shape[2]
 
     @pl.when(pl.program_id(0) == 0)
     def _():
-        def filter_item(item, _):
-            for angle in range(angles):
-                lines = sino_ref[item, angle * length : (angle + 1) * length, :]
-                line_rows = lax.dot_general(
-                    lines.T, ramp_ref[...], (((1,), (0,)), ((), ())),
-                    precision=lax.Precision.HIGHEST, preferred_element_type=jnp.float32,
-                )
-                filtered[
-                    pl.ds(pl.multiple_of(item * width, width), width),
-                    angle * length : (angle + 1) * length,
-                ] = line_rows.astype(jnp.bfloat16)
+        ramp_high = ramp_ref[...].astype(jnp.bfloat16)
+        ramp_low = (ramp_ref[...] - ramp_high.astype(jnp.float32)).astype(jnp.bfloat16)
+
+        def turn_item(item, _):
+            rows = pl.ds(pl.multiple_of(item * width, width), width)
+            turned = sino_ref[item].T
+            turned_high = turned.astype(jnp.bfloat16)
+            high[rows, :] = turned_high
+            low[rows, :] = (turned - turned_high.astype(jnp.float32)).astype(jnp.bfloat16)
             return 0
 
-        lax.fori_loop(0, items, filter_item, 0)
+        lax.fori_loop(0, items, turn_item, 0)
+        for angle in range(angles):
+            lines = slice(angle * length, (angle + 1) * length)
+            total = jnp.dot(high[:, lines], ramp_high, preferred_element_type=jnp.float32)
+            total += jnp.dot(high[:, lines], ramp_low, preferred_element_type=jnp.float32)
+            total += jnp.dot(low[:, lines], ramp_high, preferred_element_type=jnp.float32)
+            filtered[:, lines] = total.astype(jnp.bfloat16)
 
     columns = out_ref.shape[2]
     positions = lax.broadcasted_iota(jnp.int32, (length, columns), 0).astype(jnp.float32)
@@ -406,7 +418,7 @@
             pl.BlockSpec((angles, block), lambda j: (0, j)),
         ],
         out_specs=pl.BlockSpec((items, width, block), lambda j: (0, 0, j)),
-        scratch_shapes=[pltpu.VMEM((items * width, frame_count), jnp.bfloat16)],
+        scratch_shapes=[pltpu.VMEM((items * width, frame_count), jnp.bfloat16)] * 3,
         compiler_params=pltpu.CompilerParams(vmem_limit_bytes=48 * MIB),
         cost_estimate=pl.CostEstimate(
             flops=2 * items * width * frame_count * column_count,

time: 316 us -> 298 us (0.943)
  the two profiles are of different devices: /device:TPU:31 before, /device:TPU:9 now
where the time goes in v2:
time: 298 us
  Pallas kernels  292 us (98%)
  other arithmetic  3.07 us (1%)
    pallas_call x1, Pallas kernels, exchange(): pl.pallas_call(functools.partial(exchange_kernel, plan), out_shape=jax.Sh...  240 us
    pallas_call x1, Pallas kernels, project(): pl.pallas_call(functools.partial(project_kernel, angles, items), out_shap...  27.5 us
    pallas_call x1, Pallas kernels, split(): pl.pallas_call(functools.partial(split_kernel, splits), out_shape=jax.Sha...  23.9 us

profile of v2, /device:TPU:9, one launch (start us, length us, event | category | flops | bytes accessed | tf_op | source)
XLA Modules:
  0.0 297.9 jit_solution(2182855205418209649)
XLA Ops:
  0.0 0.1 pad_add_fusion
  0.1 0.1 broadcast_add_fusion
  0.2 0.7 fusion.16
  0.9 0.1 broadcast_multiply_fusion.1
  1.0 0.1 broadcast_multiply_fusion
  1.0 0.8 fusion.17
  1.8 0.6 gather_fusion
  2.5 0.5 constant_dynamic-slice_fusion
  3.0 1.3 fusion.14.place_ref
  4.3 0.1 broadcast_subtract_fusion
  4.4 0.1 sub.69
  4.5 0.1 add_bitcast_fusion
  4.6 0.1 copy.10
  4.6 0.8 copy.8.monitor_ref
  5.4 0.6 select_select_fusion.ramp_ref
  6.0 23.9 %shard_map.64 = f32[96,256,128]{2,1,0:T(8,128)} custom-call(s32[96]{0:T(128)S(1)} %fusion.14.place_ref, bf16[256,12288]{1,0:T(8,128)(2,1)} %frames_ref.1, bf16[96,512,128]{2,1,0:T(8,128)(2,1)} %weights_ref.1, f32[256,1]{1,0:T(8,128)S(1)} %copy.8.monitor_ref), custom_call_target="tpu_custom_call" | custom-call | flops 3221225472 | bytes 31457280 | tf_op jit(solution)/shard_map/pallas_call | solution.py:66
  30.0 240.5 %shard_map.65.sino_ref = f32[8,1024,128]{2,1,0:T(8,128)S(1)} custom-call(s32[384]{0:T(512)S(1)} %fusion.8.rank_ref, f32[2,4,12,256,128]{4,3,2,1,0:T(8,128)} %bitcast.28), custom_call_target="tpu_custom_call" | custom-call | flops 3145728 | bytes 25165824 | tf_op jit(solution)/shard_map/pallas_call | solution.py:331
  270.4 27.5 %shard_map.66 = bf16[8,128,8192]{2,1,0:T(8,128)(2,1)} custom-call(f32[8,1024,128]{2,1,0:T(8,128)S(1)} %shard_map.65.sino_ref, f32[512,512]{1,0:T(8,128)S(1)} %select_select_fusion.ramp_ref, f32[2,8192]{1,0:T(2,128)S(1)} %bitcast.27), custom_call_target="tpu_custom_call" | custom-call | flops 17179869184 | bytes 20971520 | tf_op jit(solution)/shard_map/pallas_call | solution.py:411
  (7 shorter events, 0.1 us)
